TPU v7x, 32 devices: a whole 2x2x4 slice. The times are simulated.
32 devices in a mesh: ep: 8 (over y, x, core), ex: 4 (over z).
Axes of the slice: x: 2, y: 2, z: 4, core: 2. Of those that a mesh axis runs over, the one named last changes fastest.
Arguments:
- dout: bfloat16 [1024, 7168], P(('ep', 'ex')), may hold values from -1.5 to 1.5
- gates: bfloat16 [1024, 8], P(('ep', 'ex')), may hold values from 0.049804688 to 0.59765625
- saved_down_input: bfloat16 [1024, 8, 1024], P(('ep', 'ex')), may hold values from -3 to 3
- routing: int32 [1024, 8], P(('ep', 'ex')), may hold values from 0 to 27, as said below
- placement: int32 [32], replicated, may hold values from 0 to 27, as said below
- partner: int32 [32], replicated, may hold values from 0 to 31, as said below
- frozen: bfloat16 [32, 1024, 7168], P(('ep', 'ex')), as said below
- colscale: float32 [32, 7168], P(('ep', 'ex')), may hold values from 0.5 to 2, as said below
- adapter_down_factor: bfloat16 [32, 1024, 64], P(('ep', 'ex')), as said below
- adapter_up_factor: bfloat16 [32, 64, 7168], P(('ep', 'ex')), as said below
- first_moment_down: bfloat16 [32, 1024, 64], P(('ep', 'ex')), as said below
- second_moment_down: bfloat16 [32, 1024, 64], P(('ep', 'ex')), may hold values from 0.1 to 4, as said below
- first_moment_up: bfloat16 [32, 64, 7168], P(('ep', 'ex')), as said below
- second_moment_up: bfloat16 [32, 64, 7168], P(('ep', 'ex')), may hold values from 0.1 to 4, as said below
Outputs:
- routed_input_gradient: bfloat16 [1024, 8, 1024], P(('ep', 'ex'))
- combine_gate_gradient: bfloat16 [1024, 8], P(('ep', 'ex'))
- updated_down_factor: bfloat16 [32, 1024, 64], P(('ep', 'ex'))
- updated_up_factor: bfloat16 [32, 64, 7168], P(('ep', 'ex'))
- updated_first_moment_down: bfloat16 [32, 1024, 64], P(('ep', 'ex'))
- updated_second_moment_down: bfloat16 [32, 1024, 64], P(('ep', 'ex'))
- updated_first_moment_up: bfloat16 [32, 64, 7168], P(('ep', 'ex'))
- updated_second_moment_up: bfloat16 [32, 64, 7168], P(('ep', 'ex'))
Inputs may be any that keep to these rules, and one draw needn't show every extreme that they name: `routing`: each token names 8 different experts. Of each device's tokens, an expert with two slots is named by exactly 16, every other expert by exactly 8. `placement`: every expert is held by one slot, or by two slots of one expert group (equal index along ep); 4 experts hold two slots, each in a group of its own. placement[partner[s]] = placement[s]; partner[s] is the other slot of the same expert, or s if the expert holds one slot. `frozen`: slots of the same expert hold equal values. `colscale`: slots of the same expert hold equal values. `adapter_down_factor`: slots of the same expert hold equal values. `adapter_up_factor`: slots of the same expert hold equal values. `first_moment_down`: slots of the same expert hold equal values. `second_moment_down`: slots of the same expert hold equal values. `first_moment_up`: slots of the same expert hold equal values. `second_moment_up`: slots of the same expert hold equal values.
All inputs are finite; a program needn't handle non-finite values.
Results may differ from a plain program's by a relative error of at most 0.005.
Values may be sent and summed in bfloat16 or wider, within the bound.
No kernel may reach another device: no remote copies, remote signals or barrier semaphores. Data moves between devices by JAX's collectives and lax.ppermute only.
A program may use at most 128 MiB of HBM per device.

v0:
```python
import jax
import jax.numpy as jnp
from jax import lax
from jax.sharding import PartitionSpec as P

adapter_scale = 2.0
beta_one = 0.9
beta_two = 0.999
adam_eps = 1e-08
learn_rate = 0.01
weight_decay = 0.01
adam_step = 10


def expert_row_block(
    hidden_row_block,
    output_gradient_rows,
    gate_row_values,
    frozen_w,
    scale,
    adapter_down_projected,
    low_b,
):
    gate_broadcast_wide = gate_row_values.astype(jnp.float32)[:, None]
    dout_wide = output_gradient_rows.astype(jnp.float32)
    adapter_output_gradient = (gate_broadcast_wide * dout_wide).astype(jnp.bfloat16)
    dsc_low = (dout_wide * scale[None, :]).astype(jnp.bfloat16)
    backward_through_adapter = jnp.dot(
        adapter_output_gradient, low_b.T, preferred_element_type=jnp.float32
    ).astype(jnp.bfloat16)
    backward_through_frozen = jnp.dot(dsc_low, frozen_w.T, preferred_element_type=jnp.float32)
    incoming_input_gradient = (
        gate_broadcast_wide * backward_through_frozen
        + adapter_scale
        * jnp.dot(
            backward_through_adapter, adapter_down_projected.T, preferred_element_type=jnp.float32
        )
    )
    adapter_down_product = jnp.dot(
        hidden_row_block, adapter_down_projected, preferred_element_type=jnp.float32
    ).astype(jnp.bfloat16)
    output_gradient_adapter = jnp.dot(
        output_gradient_rows, low_b.T, preferred_element_type=jnp.float32
    )
    gated_output = jnp.sum(
        hidden_row_block.astype(jnp.float32) * backward_through_frozen, axis=1
    ) + adapter_scale * jnp.sum(
        adapter_down_product.astype(jnp.float32) * output_gradient_adapter, axis=1
    )
    down_factor_gradient = adapter_scale * jnp.dot(
        hidden_row_block.T, backward_through_adapter, preferred_element_type=jnp.float32
    )
    up_factor_gradient = adapter_scale * jnp.dot(
        adapter_down_product.T, adapter_output_gradient, preferred_element_type=jnp.float32
    )
    return (
        incoming_input_gradient.astype(jnp.bfloat16),
        gated_output.astype(jnp.bfloat16),
        down_factor_gradient,
        up_factor_gradient,
    )


def apply_adam_update(weights, moment, second_moment, gradient):
    weights_wide = weights.astype(jnp.float32)
    first = beta_one * moment.astype(jnp.float32) + (1.0 - beta_one) * gradient
    second = beta_two * second_moment.astype(jnp.float32) + (1.0 - beta_two) * gradient * gradient
    first_hat = first / (1.0 - beta_one**adam_step)
    second_hat = second / (1.0 - beta_two**adam_step)
    fresh = weights_wide - learn_rate * (
        first_hat / (jnp.sqrt(second_hat) + adam_eps) + weight_decay * weights_wide
    )
    return (fresh.astype(jnp.bfloat16), first.astype(jnp.bfloat16), second.astype(jnp.bfloat16))


def per_device(
    dout,
    gates,
    saved_down_input,
    routing,
    placement,
    partner,
    frozen,
    colscale,
    adapter_down_factor,
    adapter_up_factor,
    first_moment_down,
    second_moment_down,
    first_moment_up,
    second_moment_up,
):
    groups = lax.axis_size("ep")
    members = lax.axis_size("ex")
    slot_count = groups * members
    tok_rows, top_count = routing.shape
    model_width = dout.shape[1]
    hidden = saved_down_input.shape[2]
    adapter_rank_width = adapter_down_factor.shape[2]
    row_count = tok_rows * top_count
    capacity = row_count // slot_count
    expert_flat = routing.reshape(row_count)
    slot_ids = jnp.arange(slot_count, dtype=jnp.int32)
    holds_expert = placement[None, :] == expert_flat[:, None]
    first_slot = jnp.min(jnp.where(holds_expert, slot_ids[None, :], slot_count), axis=1)
    last_slot = jnp.max(jnp.where(holds_expert, slot_ids[None, :], -1), axis=1)
    row_ids = jnp.arange(row_count, dtype=jnp.int32)
    earlier = row_ids[None, :] < row_ids[:, None]
    same_expert = expert_flat[None, :] == expert_flat[:, None]
    turn_index = jnp.sum((same_expert & earlier).astype(jnp.int32), axis=1)
    target = jnp.where(turn_index % 2 == 1, last_slot, first_slot)
    same_slot = target[None, :] == target[:, None]
    position = jnp.sum((same_slot & earlier).astype(jnp.int32), axis=1)
    buffer_row = target * capacity + position
    row_width = model_width + hidden
    row_data = jnp.concatenate(
        [jnp.broadcast_to(dout[:, None, :], (tok_rows, top_count, model_width)), saved_down_input],
        axis=2,
    ).reshape(row_count, row_width)
    outgoing = (
        jnp.zeros((slot_count * capacity, row_width), jnp.bfloat16).at[buffer_row].set(row_data)
    )
    outgoing_gate = (
        jnp.zeros((slot_count * capacity,), jnp.bfloat16)
        .at[buffer_row]
        .set(gates.reshape(row_count))
    )
    incoming, incoming_gate = (
        lax.all_to_all(
            outgoing.reshape(slot_count, capacity, row_width),
            ("ep", "ex"),
            split_axis=0,
            concat_axis=0,
            tiled=True,
        ),
        lax.all_to_all(
            outgoing_gate.reshape(slot_count, capacity),
            ("ep", "ex"),
            split_axis=0,
            concat_axis=0,
            tiled=True,
        ),
    )
    live_rows = slot_count * capacity
    incoming = incoming.reshape(live_rows, row_width)
    output_gradient_rows = incoming[:, :model_width]
    hidden_row_block = incoming[:, model_width:]
    incoming_input_gradient, gated_output, down_factor_gradient, up_factor_gradient = (
        expert_row_block(
            hidden_row_block,
            output_gradient_rows,
            incoming_gate.reshape(live_rows),
            frozen[0],
            colscale[0],
            adapter_down_factor[0],
            adapter_up_factor[0],
        )
    )
    returned_grad, returned_gate = (
        lax.all_to_all(
            incoming_input_gradient.reshape(slot_count, capacity, hidden),
            ("ep", "ex"),
            split_axis=0,
            concat_axis=0,
            tiled=True,
        ),
        lax.all_to_all(
            gated_output.reshape(slot_count, capacity),
            ("ep", "ex"),
            split_axis=0,
            concat_axis=0,
            tiled=True,
        ),
    )
    routed_input_gradient = returned_grad.reshape(live_rows, hidden)[buffer_row].reshape(
        tok_rows, top_count, hidden
    )
    combine_gate_gradient = returned_gate.reshape(live_rows)[buffer_row].reshape(
        tok_rows, top_count
    )
    own_member = lax.axis_index("ex")
    own_slot = lax.axis_index("ep") * members + own_member
    mate_slot = jnp.sum(jnp.where(slot_ids == own_slot, partner, 0))
    mate_member = mate_slot % members
    flat_a = down_factor_gradient.reshape(1, hidden * adapter_rank_width // 128, 128)
    flat_b = up_factor_gradient.reshape(1, adapter_rank_width, model_width)
    pieces = (
        lax.all_gather(flat_a.astype(jnp.bfloat16), "ex", axis=0, tiled=True).astype(jnp.float32),
        lax.all_gather(flat_b.astype(jnp.bfloat16), "ex", axis=0, tiled=True).astype(jnp.float32),
    )
    length = pieces[0].shape[0]
    members_here = jnp.arange(length, dtype=jnp.int32)
    chosen = ((members_here == own_member) | (members_here == mate_member)).astype(jnp.float32)
    summed_down_gradient = jnp.zeros(flat_a.shape[1:], jnp.float32) + jnp.sum(
        chosen[:, None, None] * pieces[0], axis=0
    )
    summed_up_gradient = jnp.zeros(flat_b.shape[1:], jnp.float32) + jnp.sum(
        chosen[:, None, None] * pieces[1], axis=0
    )
    summed_down_gradient = summed_down_gradient.reshape(1, hidden, adapter_rank_width)
    summed_up_gradient = summed_up_gradient.reshape(1, adapter_rank_width, model_width)
    updated_down_factor, updated_first_moment_down, updated_second_moment_down = apply_adam_update(
        adapter_down_factor, first_moment_down, second_moment_down, summed_down_gradient
    )
    updated_up_factor, updated_first_moment_up, updated_second_moment_up = apply_adam_update(
        adapter_up_factor, first_moment_up, second_moment_up, summed_up_gradient
    )
    return (
        routed_input_gradient,
        combine_gate_gradient,
        updated_down_factor,
        updated_up_factor,
        updated_first_moment_down,
        updated_second_moment_down,
        updated_first_moment_up,
        updated_second_moment_up,
    )


def solution(mesh):
    placed = (
        P(("ep", "ex"), None),
        P(("ep", "ex"), None),
        P(("ep", "ex"), None, None),
        P(("ep", "ex"), None),
        P(),
        P(),
        P(("ep", "ex"), None, None),
        P(("ep", "ex"), None),
        P(("ep", "ex"), None, None),
        P(("ep", "ex"), None, None),
        P(("ep", "ex"), None, None),
        P(("ep", "ex"), None, None),
        P(("ep", "ex"), None, None),
        P(("ep", "ex"), None, None),
    )
    return jax.shard_map(
        per_device,
        mesh=mesh,
        in_specs=placed,
        out_specs=(
            P(("ep", "ex"), None, None),
            P(("ep", "ex"), None),
            P(("ep", "ex"), None, None),
            P(("ep", "ex"), None, None),
            P(("ep", "ex"), None, None),
            P(("ep", "ex"), None, None),
            P(("ep", "ex"), None, None),
            P(("ep", "ex"), None, None),
        ),
        check_vma=False,
    )
```

profile of v0, /device:TPU:0, one launch (start us, length us, event | category | flops | bytes accessed | tf_op | source)
XLA Modules:
  0.0 243.8 jit_solution(11940484604645975405)
XLA Ops:
  7.2 0.8 copy.56
  8.0 0.1 eq.91
  8.1 0.2 convert_reduce_fusion.1
  8.3 0.8 fusion.49
  9.0 0.2 convert_reduce_fusion
  9.2 0.8 copy.57
  10.0 0.1 reshape.303
  10.1 2.2 scatter_custom_fusion
  12.3 0.7 all_to_all.21
  13.0 7.3 %all-to-all-start = ((bf16[32,1,8]{2,1,0:T(2,128)(2,1)}), bf16[32,1,8]{2,1,0:T(2,128)(2,1)S(1)}, u32[]{:S(2)}, u32[]{:S(2)}) async-start(bf16[32,1,8]{2,1,0:T(2,128)(2,1)} %all_to_all.21), calls=%async_computation | async-start | bytes 32768 | tf_op jit(solution)/shard_map/all_to_all | solution.py:135
  20.3 3.3 %broadcast_in_dim.56 = bf16[32,8,7168]{2,1,0:T(8,128)(2,1)} broadcast(bf16[32,7168]{1,0:T(8,128)(2,1)} %param.14), dimensions={0,2} | broadcast | bytes 4128768 | tf_op jit(solution)/shard_map/broadcast_in_dim | solution.py:116
  23.6 10.0 %scatter_custom_fusion.1 = bf16[256,8192]{1,0:T(8,128)(2,1)} fusion(s32[256]{0:T(256)S(1)} %bitcast.56, bf16[32,8,1024]{2,1,0:T(8,128)(2,1)S(1)} %copy-done.3, bf16[]{:T(256)} %constant.102, bf16[32,8,7168]{2,1,0:T(8,128)(2,1)} %broadcast_in_dim.56, bf16[]{:T(256)} %constant.25.clone.1), kind=kCustom, calls=%fused_computation.15 | custom fusion | flops 8388608 | bytes 8388612 | tf_op jit(solution)/shard_map/scatter | solution.py:120
  33.6 6.0 %all-to-all-start.1 = ((bf16[32,8,8192]{2,1,0:T(8,128)(2,1)}), bf16[32,8,8192]{2,1,0:T(8,128)(2,1)}, u32[]{:S(2)}, u32[]{:S(2)}) async-start(bf16[32,8,8192]{2,1,0:T(8,128)(2,1)} %bitcast.49), calls=%async_computation.1 | async-start | bytes 8388608 | tf_op jit(solution)/shard_map/all_to_all | solution.py:128
  39.6 0.2 all-gather.3.cloned.1.call-start
  39.8 0.1 convert_reduce_fusion.2
  39.9 0.1 reshape.282
  39.9 91.9 %all-to-all-done.1 = bf16[32,8,8192]{2,1,0:T(8,128)(2,1)} async-done(((bf16[32,8,8192]{2,1,0:T(8,128)(2,1)}), bf16[32,8,8192]{2,1,0:T(8,128)(2,1)}, u32[]{:S(2)}, u32[]{:S(2)}) %all-to-all-start.1) | async-done | bytes 4194336 | tf_op jit(solution)/shard_map/all_to_all | solution.py:128
  131.8 1.3 convolution_convert_fusion
  133.1 0.0 copy-start.8
  133.2 4.1 %fusion.2 = bf16[64,7168]{1,0:T(8,128)(2,1)} fusion(bf16[256,64]{0,1:T(8,128)(2,1)S(1)} %convolution_convert_fusion, f32[256]{0:T(256)S(1)} %reshape.282, bf16[256,8192]{1,0:T(8,128)(2,1)} %bitcast.7), kind=kOutput, calls=%fused_computation.9 | convolution fusion | flops 241303552 | bytes 4621312 | tf_op jit(solution)/shard_map/dot_general | solution.py:53
  137.2 0.0 all-gather.3.cloned.1.call-update
  137.3 0.6 fusion.52
  139.9 3.3 %fusion.27 = f32[256]{0:T(256)S(1)} fusion(bf16[256,8192]{1,0:T(8,128)(2,1)} %bitcast.7, bf16[1,64,7168]{2,1,0:T(8,128)(2,1)S(1)} %copy-done, bf16[256,64]{0,1:T(8,128)(2,1)S(1)} %convolution_convert_fusion), kind=kOutput, calls=%fused_computation.41 | convolution fusion | flops 234929920 | bytes 4621312 | tf_op jit(solution)/shard_map/dot_general | solution.py:42
  143.2 11.3 %multiply_reduce_fusion.1 = (f32[256]{0:T(256)S(1)}, f32[256,1024]{1,0:T(8,128)S(1)}) fusion(bf16[256,8192]{1,0:T(8,128)(2,1)} %bitcast.7, bf16[1,1024,7168]{2,1,0:T(8,128)(2,1)} %param.20, f32[7168]{0:T(1024)S(1)} %bitcast.59), kind=kOutput, calls=%fused_computation.44 | convolution fusion | flops 3764387584 | bytes 19952640 | tf_op jit(solution)/shard_map/dot_general | solution.py:31
  154.4 0.7 convert_element_type.158
  155.1 5.4 %all-to-all-start.3 = ((bf16[32,1,8]{2,1,0:T(2,128)(2,1)}), bf16[32,1,8]{2,1,0:T(2,128)(2,1)S(1)}, u32[]{:S(2)}, u32[]{:S(2)}) async-start(bf16[32,1,8]{2,1,0:T(2,128)(2,1)} %convert_element_type.158), calls=%async_computation.3 | async-start | bytes 32768 | tf_op jit(solution)/shard_map/all_to_all | solution.py:166
  160.5 3.3 %convolution_convert_fusion.1 = bf16[256,64]{0,1:T(8,128)(2,1)S(1)} fusion(f32[256]{0:T(256)S(1)} %reshape.282, bf16[256,8192]{1,0:T(8,128)(2,1)} %bitcast.7, bf16[1,64,7168]{2,1,0:T(8,128)(2,1)S(1)} %copy-done), kind=kOutput, calls=%fused_computation.40 | convolution fusion | flops 240402432 | bytes 4621312 | tf_op jit(solution)/shard_map/dot_general | solution.py:28
  163.9 0.0 copy-start.6
  163.9 1.1 fusion.22
  165.0 2.9 %all-to-all-done.3 = bf16[32,1,8]{2,1,0:T(2,128)(2,1)S(1)} async-done(((bf16[32,1,8]{2,1,0:T(2,128)(2,1)}), bf16[32,1,8]{2,1,0:T(2,128)(2,1)S(1)}, u32[]{:S(2)}, u32[]{:S(2)}) %all-to-all-start.3) | async-done | bytes 544 | tf_op jit(solution)/shard_map/all_to_all | solution.py:166
  167.9 3.0 %all-to-all-start.2 = ((bf16[32,8,1024]{2,1,0:T(8,128)(2,1)}), bf16[32,8,1024]{2,1,0:T(8,128)(2,1)S(1)}, u32[]{:S(2)}, u32[]{:S(2)}) async-start(bf16[32,8,1024]{2,1,0:T(8,128)(2,1)} %fusion.22), calls=%async_computation.2 | async-start | bytes 1048576 | tf_op jit(solution)/shard_map/all_to_all | solution.py:159
  170.9 1.3 fusion.23
  172.1 0.2 copy.60
  172.3 0.2 convert_element_type.141
  172.5 41.9 %all_gather.6 = bf16[4,512,128]{2,1,0:T(8,128)(2,1)S(1)} all-gather(bf16[1,512,128]{2,1,0:T(8,128)(2,1)S(1)} %convert_element_type.141), channel_id=1, replica_groups=mesh['ep'=8,'ex'=4] {'ex'}, dimensions={0}, use_global_device_ids=true | all-gather | bytes 655360 | tf_op jit(solution)/shard_map/all_gather | solution.py:187
  214.4 0.2 multiply_reduce_fusion
  214.6 0.1 reshape.281
  214.7 0.2 copy.61
  214.9 1.0 fusion.45
  216.0 0.1 reduce.1
  216.0 0.1 reshape.279
  216.1 1.9 gather_fusion.1
  218.0 0.1 reshape.280
  218.1 0.7 copy.64
  218.8 2.0 gather_fusion
  220.7 9.4 %all-gather.3.cloned.1.call-done = bf16[256,7168]{1,0:T(8,128)(2,1)} async-done(((bf16[64,7168]{1,0:T(8,128)(2,1)}), bf16[256,7168]{1,0:T(8,128)(2,1)}) %all-gather.3.cloned.1.call-update) | async-done | bytes 3670032 | tf_op jit(solution)/shard_map/all_gather | solution.py:188
  230.2 3.1 %fusion.5 = f32[64,7168]{1,0:T(8,128)S(1)} fusion(bf16[4,64,7168]{2,1,0:T(8,128)(2,1)} %bitcast.50, f32[4]{0:T(128)S(1)} %or_convert_fusion), kind=kLoop, calls=%fused_computation.13 | loop fusion | flops 5046272 | bytes 5505040 | tf_op jit(solution)/shard_map/reduce_sum | solution.py:196
  233.3 3.7 %fusion.33 = (bf16[1,64,7168]{2,1,0:T(8,128)(2,1)}, bf16[1,64,7168]{2,1,0:T(8,128)(2,1)}, bf16[1,64,7168]{2,1,0:T(8,128)(2,1)}) fusion(f32[64,7168]{1,0:T(8,128)S(1)} %fusion.5, bf16[1,64,7168]{2,1,0:T(8,128)(2,1)S(1)} %copy-done.1, bf16[1,64,7168]{2,1,0:T(8,128)(2,1)S(1)} %copy-done.2, bf16[1,64,7168]{2,1,0:T(8,128)(2,1)S(1)} %copy-done), kind=kLoop, calls=%fused_computation.45 | loop fusion | flops 9633792 | bytes 7340032 | tf_op jit(solution)/shard_map/convert_element_type | solution.py:73
  (23 shorter events, 0.1 us)
Async XLA Ops:
  7.2 16.5 %copy-start.3 = (bf16[32,8,1024]{2,1,0:T(8,128)(2,1)S(1)}, bf16[32,8,1024]{2,1,0:T(8,128)(2,1)}, u32[]{:S(2)}) copy-start(bf16[32,8,1024]{2,1,0:T(8,128)(2,1)} %param.16) | copy-start | bytes 1572868
  13.0 20.6 %all-to-all-start = ((bf16[32,1,8]{2,1,0:T(2,128)(2,1)}), bf16[32,1,8]{2,1,0:T(2,128)(2,1)S(1)}, u32[]{:S(2)}, u32[]{:S(2)}) async-start(bf16[32,1,8]{2,1,0:T(2,128)(2,1)} %all_to_all.21), calls=%async_computation | async-start | bytes 32768 | tf_op jit(solution)/shard_map/all_to_all | solution.py:135
  33.6 98.2 %copy-start.4 = (bf16[1,1024,64]{1,2,0:T(8,128)(2,1)S(1)}, bf16[1,1024,64]{1,2,0:T(8,128)(2,1)}, u32[]{:S(2)}) copy-start(bf16[1,1024,64]{1,2,0:T(8,128)(2,1)} %param.22) | copy-start | bytes 393220
  33.6 98.2 %all-to-all-start.1 = ((bf16[32,8,8192]{2,1,0:T(8,128)(2,1)}), bf16[32,8,8192]{2,1,0:T(8,128)(2,1)}, u32[]{:S(2)}, u32[]{:S(2)}) async-start(bf16[32,8,8192]{2,1,0:T(8,128)(2,1)} %bitcast.49), calls=%async_computation.1 | async-start | bytes 8388608 | tf_op jit(solution)/shard_map/all_to_all | solution.py:128
  39.6 190.6 %all-gather.3.cloned.1.call-start = ((), (), s32[]{:S(2)}) async-start(), calls=%async_computation.4 | async-start | bytes 4587520 | tf_op jit(solution)/shard_map/all_gather | solution.py:188
  133.1 4.1 %copy-start.8 = (s32[32]{0:T(128)S(1)}, s32[32]{0:T(128)}, u32[]{:S(2)}) copy-start(s32[32]{0:T(128)} %param.19) | copy-start | bytes 388
  133.1 6.7 %copy-start = (bf16[1,64,7168]{2,1,0:T(8,128)(2,1)S(1)}, bf16[1,64,7168]{2,1,0:T(8,128)(2,1)}, u32[]{:S(2)}) copy-start(bf16[1,64,7168]{2,1,0:T(8,128)(2,1)} %param.23) | copy-start | bytes 2752516
  137.2 5.9 %copy-start.7 = (f32[1,7168]{1,0:T(1,128)S(1)}, f32[1,7168]{1,0:T(1,128)}, u32[]{:S(2)}) copy-start(f32[1,7168]{1,0:T(1,128)} %param.21) | copy-start | bytes 86020
  155.1 12.7 %all-to-all-start.3 = ((bf16[32,1,8]{2,1,0:T(2,128)(2,1)}), bf16[32,1,8]{2,1,0:T(2,128)(2,1)S(1)}, u32[]{:S(2)}, u32[]{:S(2)}) async-start(bf16[32,1,8]{2,1,0:T(2,128)(2,1)} %convert_element_type.158), calls=%async_computation.3 | async-start | bytes 32768 | tf_op jit(solution)/shard_map/all_to_all | solution.py:166
  163.9 51.0 %copy-start.5 = (bf16[1,1024,64]{1,2,0:T(8,128)(2,1)S(1)}, bf16[1,1024,64]{1,2,0:T(8,128)(2,1)}, u32[]{:S(2)}) copy-start(bf16[1,1024,64]{1,2,0:T(8,128)(2,1)} %param.25) | copy-start | bytes 393220
  163.9 51.0 %copy-start.6 = (bf16[1,1024,64]{1,2,0:T(8,128)(2,1)S(1)}, bf16[1,1024,64]{1,2,0:T(8,128)(2,1)}, u32[]{:S(2)}) copy-start(bf16[1,1024,64]{1,2,0:T(8,128)(2,1)} %param.24) | copy-start | bytes 393220
  167.9 50.9 %all-to-all-start.2 = ((bf16[32,8,1024]{2,1,0:T(8,128)(2,1)}), bf16[32,8,1024]{2,1,0:T(8,128)(2,1)S(1)}, u32[]{:S(2)}, u32[]{:S(2)}) async-start(bf16[32,8,1024]{2,1,0:T(8,128)(2,1)} %fusion.22), calls=%async_computation.2 | async-start | bytes 1048576 | tf_op jit(solution)/shard_map/all_to_all | solution.py:159
  220.7 12.5 %copy-start.1 = (bf16[1,64,7168]{2,1,0:T(8,128)(2,1)S(1)}, bf16[1,64,7168]{2,1,0:T(8,128)(2,1)}, u32[]{:S(2)}) copy-start(bf16[1,64,7168]{2,1,0:T(8,128)(2,1)} %param.27) | copy-start | bytes 2752516
  220.7 12.5 %copy-start.2 = (bf16[1,64,7168]{2,1,0:T(8,128)(2,1)S(1)}, bf16[1,64,7168]{2,1,0:T(8,128)(2,1)}, u32[]{:S(2)}) copy-start(bf16[1,64,7168]{2,1,0:T(8,128)(2,1)} %param.26) | copy-start | bytes 2752516
Sparse Core Ops, SparseCore 0:
  137.4 92.7 all-gather.2
where the time goes:
time: 244 us
  waiting for transfers between devices  104 us (43%)
  blocking collectives  41.9 us (17%)
  matrix products  25.6 us (10%)
  starting transfers between devices  21.8 us (9%)
  other arithmetic  19.9 us (8%)
  between operations  16.2 us (7%)
  local copies, waits for them, and re-layouts  14.2 us (6%)
    all_to_all x1, waiting for transfers between devices, per_device(): lax.all_to_all(outgoing.reshape(slot_count, capacity, row_width), ('ep',...  91.9 us
    all_gather x1, blocking collectives, per_device(): lax.all_gather(flat_a.astype(jnp.bfloat16), 'ex', axis=0, tiled=True)  41.9 us
    dot_general x1, matrix products, expert_row_block(): jnp.dot(dsc_low, frozen_w.T, preferred_element_type=jnp.float32)  11.3 us
    scatter x1, other arithmetic, per_device(): jnp.zeros((slot_count * capacity, row_width), jnp.bfloat16).at[buffer_row]  9.96 us
    all_gather x1, waiting for transfers between devices, per_device(): lax.all_gather(flat_b.astype(jnp.bfloat16), 'ex', axis=0, tiled=True)  9.41 us
    all_to_all x1, starting transfers between devices, per_device(): lax.all_to_all(outgoing_gate.reshape(slot_count, capacity), ('ep', 'ex'),...  7.3 us
    all_to_all x1, starting transfers between devices, per_device(): lax.all_to_all(outgoing.reshape(slot_count, capacity, row_width), ('ep',...  5.96 us
    all_to_all x1, starting transfers between devices, per_device(): lax.all_to_all(gated_output.reshape(slot_count, capacity), ('ep', 'ex'),...  5.36 us
  transfers between devices with their start and end apart: 5, of which 3 were waited for; matrix products, arithmetic and copies ran while one was open for 17% of the time, Pallas kernels for 0%

commit v1 on v0

--- a/solution.py
+++ b/solution.py
@@ -1,3 +1,4 @@
+import functools
 import jax
 import jax.numpy as jnp
 from jax import lax
@@ -10,6 +11,39 @@
 learn_rate = 0.01
 weight_decay = 0.01
 adam_step = 10
+
+
+def _match_run(field_in, at_axis):
+    x_now = lax.psum(1, axis_name="ex")
+    b_next = lax.axis_index("ex")
+    entries = []
+    shaped, finding, then = (x_now, b_next, field_in.shape[at_axis])
+    for p, dev_j in enumerate(field_in.shape):
+        entries.append(dev_j * shaped if p == at_axis else dev_j)
+    r1 = e_now = field_in
+    main = lax.dynamic_update_slice_in_dim(
+        jnp.zeros(entries, field_in.dtype), field_in, finding * then, axis=at_axis
+    )
+    for hop_no in range(1, shaped // 2 + 1):
+        by_rank = []
+        for p in range(shaped):
+            by_rank.append((p, (p + 1) % shaped))
+        r1 = lax.ppermute(r1, axis_name="ex", perm=by_rank)
+        main = lax.dynamic_update_slice_in_dim(
+            main, r1, (finding - hop_no) % shaped * then, axis=at_axis
+        )
+        if 2 * hop_no < shaped:
+            rows = []
+            for p in range(shaped):
+                rows.append((p, (p - 1) % shaped))
+            e_now = lax.ppermute(e_now, axis_name="ex", perm=rows)
+            main = lax.dynamic_update_slice_in_dim(
+                main, e_now, (finding + hop_no) % shaped * then, axis=at_axis
+            )
+    return main
+
+
+_draw_signs = functools.partial(_match_run, at_axis=0)
 
 
 def expert_row_block(
@@ -184,7 +218,7 @@
     flat_a = down_factor_gradient.reshape(1, hidden * adapter_rank_width // 128, 128)
     flat_b = up_factor_gradient.reshape(1, adapter_rank_width, model_width)
     pieces = (
-        lax.all_gather(flat_a.astype(jnp.bfloat16), "ex", axis=0, tiled=True).astype(jnp.float32),
+        _draw_signs(flat_a.astype(jnp.bfloat16)).astype(jnp.float32),
         lax.all_gather(flat_b.astype(jnp.bfloat16), "ex", axis=0, tiled=True).astype(jnp.float32),
     )
     length = pieces[0].shape[0]

time: 244 us -> 244 us (level)
  blocking collectives: 41.9 us -> 0 us
  waiting for transfers between devices: 104 us -> 129 us
  starting transfers between devices: 21.8 us -> 38.4 us
    all_gather x1 -> x0, blocking collectives: 41.9 us -> none  [per_device(): lax.all_gather(flat_a.astype(jnp.bfloat16), 'ex', axis=0, tiled=True)]
    ppermute x0 -> x3, waiting for transfers between devices: none -> 25.3 us  [the longest x2 25.3 us: _match_run(): r1 = lax.ppermute(r1, axis_name='ex', perm=by_rank)]
    ppermute x0 -> x3, starting transfers between devices: none -> 16.4 us  [the longest x2 14.4 us: _match_run(): r1 = lax.ppermute(r1, axis_name='ex', perm=by_rank)]
  transfers between devices with their start and end apart: 5 -> 8, of which waited for: 3 -> 5; matrix products, arithmetic and copies ran while one was open for 17% -> 17% of each run, Pallas kernels for 0% -> 0%
where the time goes in v1:
time: 244 us
  waiting for transfers between devices  129 us (53%)
  starting transfers between devices  38.4 us (16%)
  matrix products  25.7 us (11%)
  other arithmetic  19.8 us (8%)
  between operations  16.3 us (7%)
  local copies, waits for them, and re-layouts  14.3 us (6%)
    all_to_all x1, waiting for transfers between devices, per_device(): lax.all_to_all(outgoing.reshape(slot_count, capacity, row_width), ('ep',...  91.9 us
    ppermute x2, waiting for transfers between devices, _match_run(): r1 = lax.ppermute(r1, axis_name='ex', perm=by_rank)  25.3 us
    ppermute x2, starting transfers between devices, _match_run(): r1 = lax.ppermute(r1, axis_name='ex', perm=by_rank)  14.4 us
    dot_general x1, matrix products, expert_row_block(): jnp.dot(dsc_low, frozen_w.T, preferred_element_type=jnp.float32)  11.3 us
    scatter x1, other arithmetic, per_device(): jnp.zeros((slot_count * capacity, row_width), jnp.bfloat16).at[buffer_row]  9.96 us
    all_gather x1, waiting for transfers between devices, per_device(): lax.all_gather(flat_b.astype(jnp.bfloat16), 'ex', axis=0, tiled=True)  9.31 us
    all_to_all x1, starting transfers between devices, per_device(): lax.all_to_all(outgoing_gate.reshape(slot_count, capacity), ('ep', 'ex'),...  7.3 us
    all_to_all x1, starting transfers between devices, per_device(): lax.all_to_all(outgoing.reshape(slot_count, capacity, row_width), ('ep',...  5.96 us
  transfers between devices with their start and end apart: 8, of which 5 were waited for; matrix products, arithmetic and copies ran while one was open for 17% of the time, Pallas kernels for 0%

profile of v1, /device:TPU:0, one launch (start us, length us, event | category | flops | bytes accessed | tf_op | source)
XLA Modules:
  0.0 243.8 jit_solution(8940300245096639061)
XLA Ops:
  7.2 0.8 copy.56
  8.0 0.1 eq.94
  8.1 0.2 convert_reduce_fusion.1
  8.3 0.8 fusion.49
  9.0 0.2 convert_reduce_fusion
  9.2 0.8 copy.57
  10.0 0.1 reshape.303
  10.1 2.2 scatter_custom_fusion
  12.3 0.7 all_to_all.21
  13.0 7.3 %all-to-all-start = ((bf16[32,1,8]{2,1,0:T(2,128)(2,1)}), bf16[32,1,8]{2,1,0:T(2,128)(2,1)S(1)}, u32[]{:S(2)}, u32[]{:S(2)}) async-start(bf16[32,1,8]{2,1,0:T(2,128)(2,1)} %all_to_all.21), calls=%async_computation | async-start | bytes 32768 | tf_op jit(solution)/shard_map/all_to_all | solution.py:169
  20.3 3.3 %broadcast_in_dim.59 = bf16[32,8,7168]{2,1,0:T(8,128)(2,1)} broadcast(bf16[32,7168]{1,0:T(8,128)(2,1)} %param.14), dimensions={0,2} | broadcast | bytes 4128768 | tf_op jit(solution)/shard_map/broadcast_in_dim | solution.py:150
  23.6 10.0 %scatter_custom_fusion.1 = bf16[256,8192]{1,0:T(8,128)(2,1)} fusion(s32[256]{0:T(256)S(1)} %bitcast.56, bf16[32,8,1024]{2,1,0:T(8,128)(2,1)S(1)} %copy-done.3, bf16[]{:T(256)} %constant.119, bf16[32,8,7168]{2,1,0:T(8,128)(2,1)} %broadcast_in_dim.59, bf16[]{:T(256)} %constant.38.clone.1), kind=kCustom, calls=%fused_computation.15 | custom fusion | flops 8388608 | bytes 8388612 | tf_op jit(solution)/shard_map/scatter | solution.py:154
  33.6 6.0 %all-to-all-start.1 = ((bf16[32,8,8192]{2,1,0:T(8,128)(2,1)}), bf16[32,8,8192]{2,1,0:T(8,128)(2,1)}, u32[]{:S(2)}, u32[]{:S(2)}) async-start(bf16[32,8,8192]{2,1,0:T(8,128)(2,1)} %bitcast.49), calls=%async_computation.1 | async-start | bytes 8388608 | tf_op jit(solution)/shard_map/all_to_all | solution.py:162
  39.6 0.2 all-gather.3.cloned.1.call-start
  39.9 0.1 reshape.282
  39.9 91.9 %all-to-all-done.1 = bf16[32,8,8192]{2,1,0:T(8,128)(2,1)} async-done(((bf16[32,8,8192]{2,1,0:T(8,128)(2,1)}), bf16[32,8,8192]{2,1,0:T(8,128)(2,1)}, u32[]{:S(2)}, u32[]{:S(2)}) %all-to-all-start.1) | async-done | bytes 4194336 | tf_op jit(solution)/shard_map/all_to_all | solution.py:162
  131.8 1.3 convolution_convert_fusion
  133.2 4.1 %fusion.2 = bf16[64,7168]{1,0:T(8,128)(2,1)} fusion(bf16[256,64]{0,1:T(8,128)(2,1)S(1)} %convolution_convert_fusion, f32[256]{0:T(256)S(1)} %reshape.282, bf16[256,8192]{1,0:T(8,128)(2,1)} %bitcast.7), kind=kOutput, calls=%fused_computation.9 | convolution fusion | flops 241303552 | bytes 4621312 | tf_op jit(solution)/shard_map/dot_general | solution.py:87
  137.3 0.6 fusion.52
  139.9 3.3 %fusion.27 = f32[256]{0:T(256)S(1)} fusion(bf16[256,8192]{1,0:T(8,128)(2,1)} %bitcast.7, bf16[1,64,7168]{2,1,0:T(8,128)(2,1)S(1)} %copy-done, bf16[256,64]{0,1:T(8,128)(2,1)S(1)} %convolution_convert_fusion), kind=kOutput, calls=%fused_computation.41 | convolution fusion | flops 234929920 | bytes 4621312 | tf_op jit(solution)/shard_map/dot_general | solution.py:76
  143.2 11.3 %multiply_reduce_fusion.1 = (f32[256]{0:T(256)S(1)}, f32[256,1024]{1,0:T(8,128)S(1)}) fusion(bf16[256,8192]{1,0:T(8,128)(2,1)} %bitcast.7, bf16[1,1024,7168]{2,1,0:T(8,128)(2,1)} %param.20, f32[7168]{0:T(1024)S(1)} %bitcast.59), kind=kOutput, calls=%fused_computation.44 | convolution fusion | flops 3764387584 | bytes 19952640 | tf_op jit(solution)/shard_map/dot_general | solution.py:65
  154.5 0.7 convert_element_type.158
  155.2 5.3 %all-to-all-start.3 = ((bf16[32,1,8]{2,1,0:T(2,128)(2,1)}), bf16[32,1,8]{2,1,0:T(2,128)(2,1)S(1)}, u32[]{:S(2)}, u32[]{:S(2)}) async-start(bf16[32,1,8]{2,1,0:T(2,128)(2,1)} %convert_element_type.158), calls=%async_computation.3 | async-start | bytes 32768 | tf_op jit(solution)/shard_map/all_to_all | solution.py:200
  160.5 3.4 %convolution_convert_fusion.1 = bf16[256,64]{0,1:T(8,128)(2,1)S(1)} fusion(f32[256]{0:T(256)S(1)} %reshape.282, bf16[256,8192]{1,0:T(8,128)(2,1)} %bitcast.7, bf16[1,64,7168]{2,1,0:T(8,128)(2,1)S(1)} %copy-done), kind=kOutput, calls=%fused_computation.40 | convolution fusion | flops 240402432 | bytes 4621312 | tf_op jit(solution)/shard_map/dot_general | solution.py:62
  163.9 1.1 fusion.22
  165.0 2.8 %all-to-all-done.3 = bf16[32,1,8]{2,1,0:T(2,128)(2,1)S(1)} async-done(((bf16[32,1,8]{2,1,0:T(2,128)(2,1)}), bf16[32,1,8]{2,1,0:T(2,128)(2,1)S(1)}, u32[]{:S(2)}, u32[]{:S(2)}) %all-to-all-start.3) | async-done | bytes 544 | tf_op jit(solution)/shard_map/all_to_all | solution.py:200
  167.9 3.1 %all-to-all-start.2 = ((bf16[32,8,1024]{2,1,0:T(8,128)(2,1)}), bf16[32,8,1024]{2,1,0:T(8,128)(2,1)S(1)}, u32[]{:S(2)}, u32[]{:S(2)}) async-start(bf16[32,8,1024]{2,1,0:T(8,128)(2,1)} %fusion.22), calls=%async_computation.2 | async-start | bytes 1048576 | tf_op jit(solution)/shard_map/all_to_all | solution.py:193
  171.0 1.3 fusion.23
  172.2 0.2 copy.60
  172.4 0.1 convert_element_type.141
  172.6 1.8 collective-permute-start
  174.4 2.1 collective-permute-start.1
  176.4 0.1 broadcast_in_dim.61
  176.6 0.1 reshape.279
  176.7 1.9 gather_fusion.1
  178.6 0.1 reshape.280
  178.7 0.7 copy.64
  179.3 19.3 %collective-permute-done = bf16[1,512,128]{2,1,0:T(8,128)(2,1)S(1)} collective-permute-done((bf16[1,512,128]{2,1,0:T(8,128)(2,1)S(1)}, bf16[1,512,128]{2,1,0:T(8,128)(2,1)S(1)}, u32[]{:S(2)}, u32[]{:S(2)}) %collective-permute-start) | collective-permute-done | bytes 131104 | tf_op jit(solution)/shard_map/ppermute | solution.py:31
  198.7 12.5 %collective-permute-start.2 = (bf16[1,512,128]{2,1,0:T(8,128)(2,1)S(1)}, bf16[1,512,128]{2,1,0:T(8,128)(2,1)S(1)}, u32[]{:S(2)}, u32[]{:S(2)}) collective-permute-start(bf16[1,512,128]{2,1,0:T(8,128)(2,1)S(1)} %collective-permute-done), channel_id=1, source_target_pairs={{0,1},{1,2},{2,3},{3,0},{4,5},{5,6},{6,7},{7,4},{8,9},{9,10},{10,1... | collective-permute-start | bytes 393224 | tf_op jit(solution)/shard_map/ppermute | solution.py:31
  211.3 6.0 %collective-permute-done.2 = bf16[1,512,128]{2,1,0:T(8,128)(2,1)S(1)} collective-permute-done((bf16[1,512,128]{2,1,0:T(8,128)(2,1)S(1)}, bf16[1,512,128]{2,1,0:T(8,128)(2,1)S(1)}, u32[]{:S(2)}, u32[]{:S(2)}) %collective-permute-start.2) | collective-permute-done | bytes 131104 | tf_op jit(solution)/shard_map/ppermute | solution.py:31
  217.3 0.2 multiply_reduce_fusion
  217.5 0.1 reshape.281
  217.6 0.2 copy.61
  217.8 1.0 fusion.45
  218.9 2.0 gather_fusion
  220.8 9.3 %all-gather.3.cloned.1.call-done = bf16[256,7168]{1,0:T(8,128)(2,1)} async-done(((bf16[64,7168]{1,0:T(8,128)(2,1)}), bf16[256,7168]{1,0:T(8,128)(2,1)}) %all-gather.3.cloned.1.call-update) | async-done | bytes 3670032 | tf_op jit(solution)/shard_map/all_gather | solution.py:222
  230.2 3.1 %fusion.5 = f32[64,7168]{1,0:T(8,128)S(1)} fusion(bf16[4,64,7168]{2,1,0:T(8,128)(2,1)} %bitcast.50, f32[4]{0:T(128)S(1)} %or_convert_fusion), kind=kLoop, calls=%fused_computation.13 | loop fusion | flops 5046272 | bytes 5505040 | tf_op jit(solution)/shard_map/reduce_sum | solution.py:230
  233.2 3.7 %fusion.33 = (bf16[1,64,7168]{2,1,0:T(8,128)(2,1)}, bf16[1,64,7168]{2,1,0:T(8,128)(2,1)}, bf16[1,64,7168]{2,1,0:T(8,128)(2,1)}) fusion(f32[64,7168]{1,0:T(8,128)S(1)} %fusion.5, bf16[1,64,7168]{2,1,0:T(8,128)(2,1)S(1)} %copy-done.1, bf16[1,64,7168]{2,1,0:T(8,128)(2,1)S(1)} %copy-done.2, bf16[1,64,7168]{2,1,0:T(8,128)(2,1)S(1)} %copy-done), kind=kLoop, calls=%fused_computation.45 | loop fusion | flops 9633792 | bytes 7340032 | tf_op jit(solution)/shard_map/convert_element_type | solution.py:107
  (33 shorter events, 0.3 us)
Async XLA Ops:
  7.2 16.5 %copy-start.3 = (bf16[32,8,1024]{2,1,0:T(8,128)(2,1)S(1)}, bf16[32,8,1024]{2,1,0:T(8,128)(2,1)}, u32[]{:S(2)}) copy-start(bf16[32,8,1024]{2,1,0:T(8,128)(2,1)} %param.16) | copy-start | bytes 1572868
  13.0 20.6 %all-to-all-start = ((bf16[32,1,8]{2,1,0:T(2,128)(2,1)}), bf16[32,1,8]{2,1,0:T(2,128)(2,1)S(1)}, u32[]{:S(2)}, u32[]{:S(2)}) async-start(bf16[32,1,8]{2,1,0:T(2,128)(2,1)} %all_to_all.21), calls=%async_computation | async-start | bytes 32768 | tf_op jit(solution)/shard_map/all_to_all | solution.py:169
  33.6 98.2 %copy-start.4 = (bf16[1,1024,64]{1,2,0:T(8,128)(2,1)S(1)}, bf16[1,1024,64]{1,2,0:T(8,128)(2,1)}, u32[]{:S(2)}) copy-start(bf16[1,1024,64]{1,2,0:T(8,128)(2,1)} %param.22) | copy-start | bytes 393220
  33.6 98.2 %all-to-all-start.1 = ((bf16[32,8,8192]{2,1,0:T(8,128)(2,1)}), bf16[32,8,8192]{2,1,0:T(8,128)(2,1)}, u32[]{:S(2)}, u32[]{:S(2)}) async-start(bf16[32,8,8192]{2,1,0:T(8,128)(2,1)} %bitcast.49), calls=%async_computation.1 | async-start | bytes 8388608 | tf_op jit(solution)/shard_map/all_to_all | solution.py:162
  39.6 190.6 %all-gather.3.cloned.1.call-start = ((), (), s32[]{:S(2)}) async-start(), calls=%async_computation.4 | async-start | bytes 4587520 | tf_op jit(solution)/shard_map/all_gather | solution.py:222
  133.1 4.1 %copy-start.8 = (s32[32]{0:T(128)S(1)}, s32[32]{0:T(128)}, u32[]{:S(2)}) copy-start(s32[32]{0:T(128)} %param.19) | copy-start | bytes 388
  133.1 6.7 %copy-start = (bf16[1,64,7168]{2,1,0:T(8,128)(2,1)S(1)}, bf16[1,64,7168]{2,1,0:T(8,128)(2,1)}, u32[]{:S(2)}) copy-start(bf16[1,64,7168]{2,1,0:T(8,128)(2,1)} %param.23) | copy-start | bytes 2752516
  137.2 6.0 %copy-start.7 = (f32[1,7168]{1,0:T(1,128)S(1)}, f32[1,7168]{1,0:T(1,128)}, u32[]{:S(2)}) copy-start(f32[1,7168]{1,0:T(1,128)} %param.21) | copy-start | bytes 86020
  155.2 12.7 %all-to-all-start.3 = ((bf16[32,1,8]{2,1,0:T(2,128)(2,1)}), bf16[32,1,8]{2,1,0:T(2,128)(2,1)S(1)}, u32[]{:S(2)}, u32[]{:S(2)}) async-start(bf16[32,1,8]{2,1,0:T(2,128)(2,1)} %convert_element_type.158), calls=%async_computation.3 | async-start | bytes 32768 | tf_op jit(solution)/shard_map/all_to_all | solution.py:200
  165.0 52.8 %copy-start.5 = (bf16[1,1024,64]{1,2,0:T(8,128)(2,1)S(1)}, bf16[1,1024,64]{1,2,0:T(8,128)(2,1)}, u32[]{:S(2)}) copy-start(bf16[1,1024,64]{1,2,0:T(8,128)(2,1)} %param.25) | copy-start | bytes 393220
  165.0 52.8 %copy-start.6 = (bf16[1,1024,64]{1,2,0:T(8,128)(2,1)S(1)}, bf16[1,1024,64]{1,2,0:T(8,128)(2,1)}, u32[]{:S(2)}) copy-start(bf16[1,1024,64]{1,2,0:T(8,128)(2,1)} %param.24) | copy-start | bytes 393220
  167.9 51.0 %all-to-all-start.2 = ((bf16[32,8,1024]{2,1,0:T(8,128)(2,1)}), bf16[32,8,1024]{2,1,0:T(8,128)(2,1)S(1)}, u32[]{:S(2)}, u32[]{:S(2)}) async-start(bf16[32,8,1024]{2,1,0:T(8,128)(2,1)} %fusion.22), calls=%async_computation.2 | async-start | bytes 1048576 | tf_op jit(solution)/shard_map/all_to_all | solution.py:193
  172.6 26.1 %collective-permute-start = (bf16[1,512,128]{2,1,0:T(8,128)(2,1)S(1)}, bf16[1,512,128]{2,1,0:T(8,128)(2,1)S(1)}, u32[]{:S(2)}, u32[]{:S(2)}) collective-permute-start(bf16[1,512,128]{2,1,0:T(8,128)(2,1)S(1)} %convert_element_type.141), channel_id=1, source_target_pairs={{0,1},{1,2},{2,3},{3,0},{4,5},{5,6},{6,7},{7,4},{8,9},{9,10},{10,1... | collective-permute-start | bytes 393224 | tf_op jit(solution)/shard_map/ppermute | solution.py:31
  174.4 36.8 %collective-permute-start.1 = (bf16[1,512,128]{2,1,0:T(8,128)(2,1)S(1)}, bf16[1,512,128]{2,1,0:T(8,128)(2,1)S(1)}, u32[]{:S(2)}, u32[]{:S(2)}) collective-permute-start(bf16[1,512,128]{2,1,0:T(8,128)(2,1)S(1)} %convert_element_type.141), channel_id=1, source_target_pairs={{0,3},{1,0},{2,1},{3,2},{4,7},{5,4},{6,5},{7,6},{8,11},{9,8},{10,9... | collective-permute-start | bytes 393224 | tf_op jit(solution)/shard_map/ppermute | solution.py:39
  198.7 18.6 %collective-permute-start.2 = (bf16[1,512,128]{2,1,0:T(8,128)(2,1)S(1)}, bf16[1,512,128]{2,1,0:T(8,128)(2,1)S(1)}, u32[]{:S(2)}, u32[]{:S(2)}) collective-permute-start(bf16[1,512,128]{2,1,0:T(8,128)(2,1)S(1)} %collective-permute-done), channel_id=1, source_target_pairs={{0,1},{1,2},{2,3},{3,0},{4,5},{5,6},{6,7},{7,4},{8,9},{9,10},{10,1... | collective-permute-start | bytes 393224 | tf_op jit(solution)/shard_map/ppermute | solution.py:31
  220.8 12.4 %copy-start.1 = (bf16[1,64,7168]{2,1,0:T(8,128)(2,1)S(1)}, bf16[1,64,7168]{2,1,0:T(8,128)(2,1)}, u32[]{:S(2)}) copy-start(bf16[1,64,7168]{2,1,0:T(8,128)(2,1)} %param.27) | copy-start | bytes 2752516
  220.8 12.4 %copy-start.2 = (bf16[1,64,7168]{2,1,0:T(8,128)(2,1)S(1)}, bf16[1,64,7168]{2,1,0:T(8,128)(2,1)}, u32[]{:S(2)}) copy-start(bf16[1,64,7168]{2,1,0:T(8,128)(2,1)} %param.26) | copy-start | bytes 2752516
Sparse Core Ops, SparseCore 0:
  137.4 92.7 all-gather.2
